TPU v7x, 32 devices: a whole 2x2x4 slice. The times are simulated.
32 devices in a mesh: rep: 2 (over x), sec: 16 (over z, y, core).
Axes of the slice: x: 2, y: 2, z: 4, core: 2. Of those that a mesh axis runs over, the one named last changes fastest.
Arguments:
- wavefunction: bfloat16 [32, 384, 384], P(('rep', 'sec')), parts along dimension 0, may hold values from -48 to 48
- left_env: bfloat16 [32, 16, 384, 384], P(('rep', 'sec')), parts along dimension 0, may hold values from -3 to 3
- right_env: bfloat16 [32, 16, 384, 384], P(('rep', 'sec')), parts along dimension 0, may hold values from -3 to 3
- sector_sizes: int32 [16, 2], P('sec'), may hold values from 32 to 384, as said below
- term_links: int32 [16, 16], P('sec'), may hold values from 0 to 1, as said below
Outputs:
- applied_first: bfloat16 [32, 384, 384], P(('rep', 'sec')), parts along dimension 0
- applied_second: bfloat16 [32, 384, 384], P(('rep', 'sec')), parts along dimension 0
There are 2 independent parts, one for each index of `rep`. A program takes and returns all parts, laid end to end along the dimension named above; an argument that names none is the same for every part. Nothing has to cross between parts.
Inputs may be any that keep to these rules, and one draw needn't show every extreme that they name: `sector_sizes`: live rows (column 0) and live columns (column 1) of each sector, multiples of 32; one sector has 384 of both and another 32 of both. `term_links`: 0 for every hopping term whose source would leave the down-spin range 0 to 7 or the ends of the sector list.
All inputs are finite; a program needn't handle non-finite values.
Results may differ from a plain program's by a relative error of at most 0.0065.
The roundings to bfloat16 on the way count: a program that leaves them out, or rounds other values in their place, can miss the bound.
Values may be sent and summed in bfloat16 or wider, within the bound.
A program may use at most 128 MiB of HBM per device.

v0:
```python
import jax
import jax.numpy as jnp
from jax import lax
from jax.sharding import PartitionSpec as P

ONSITE = 4
HOPS = 3
ND = 8


def shifted(value, axis, by):
    devices = lax.axis_size(axis)
    pairs = [(i, i + by) for i in range(devices) if 0 <= i + by < devices]
    return lax.ppermute(value, axis, pairs)


def hop_offsets():
    return (1, -1, ND, -ND)


def live_region(size_pair, block_size):
    positions = jnp.arange(block_size, dtype=jnp.int32)
    return (positions[:, None] < size_pair[0]) & (positions[None, :] < size_pair[1])


def times_maps(vector, right_maps):
    return jnp.einsum("ic,wcd->wid", vector, right_maps, preferred_element_type=jnp.float32).astype(
        jnp.bfloat16
    )


def apply_hamiltonian(vector, left_blocks, right_blocks, links_row, region):
    term_products = [times_maps(vector, right_blocks[:ONSITE])]
    for direction, offset in enumerate(hop_offsets()):
        first_term = ONSITE + direction * HOPS
        outgoing = times_maps(vector, right_blocks[first_term : first_term + HOPS])
        term_products.append(shifted(outgoing, "sec", offset))
    stacked = jnp.concatenate(term_products, axis=0) * links_row.astype(jnp.bfloat16)[:, None, None]
    accumulated = jnp.einsum(
        "wij,wjd->id", left_blocks, stacked, preferred_element_type=jnp.float32
    )
    return jnp.where(region, accumulated, jnp.zeros((), jnp.float32)).astype(jnp.bfloat16)


def on_device(wavefunction, left_env, right_env, sector_sizes, term_links):
    block_size = wavefunction.shape[1]
    sizes_row = sector_sizes[0]
    links_row = term_links[0]
    left_blocks = left_env[0]
    right_blocks = right_env[0]
    region = live_region(sizes_row, block_size)
    first_vector = jnp.where(region, wavefunction[0], jnp.zeros((), jnp.bfloat16))
    applied_first = apply_hamiltonian(first_vector, left_blocks, right_blocks, links_row, region)
    first_values = first_vector.astype(jnp.float32)
    applied_values = applied_first.astype(jnp.float32)
    correlation, norm_first = lax.psum(
        (jnp.sum(first_values * applied_values), jnp.sum(first_values * first_values)), "sec"
    )
    rayleigh = correlation / (norm_first + 1e-06)
    residual = applied_values - rayleigh * first_values
    spread = lax.psum(jnp.sum(residual * residual), "sec")
    cell_count = lax.axis_size("sec") * block_size * block_size
    second_vector = (residual * lax.rsqrt(spread / cell_count + 1e-06)).astype(jnp.bfloat16)
    applied_second = apply_hamiltonian(second_vector, left_blocks, right_blocks, links_row, region)
    return (applied_first[None], applied_second[None])


def solution(mesh):
    return jax.shard_map(
        on_device,
        mesh=mesh,
        in_specs=(
            P(("rep", "sec"), None, None),
            P(("rep", "sec"), None, None, None),
            P(("rep", "sec"), None, None, None),
            P("sec", None),
            P("sec", None),
        ),
        out_specs=(P(("rep", "sec"), None, None), P(("rep", "sec"), None, None)),
        check_vma=False,
    )
```

profile of v0, /device:TPU:1, one launch (start us, length us, event | category | flops | bytes accessed | tf_op | source)
XLA Modules:
  0.0 204.2 jit_solution(12627166892184119720)
XLA Ops:
  0.6 0.0 copy-start
  0.6 1.3 fusion.84
  2.0 1.3 iota_compare_fusion
  3.3 0.0 copy-start.1
  3.3 3.0 %fusion.12 = bf16[3,384,384]{1,2,0:T(8,128)(2,1)} fusion(bf16[1,16,384,384]{3,2,1,0:T(8,128)(2,1)} %param.7, bf16[1,384,384]{2,1,0:T(8,128)(2,1)} %param.5, pred[384]{0:T(512)(128)(4,1)S(1)} %get-tuple-element.11, pred[384]{0:T(512)(128)(4,1)S(1)} %get-tuple-element.12), kind=kOutput, calls=%fused_computation.22 | convolution fusion | flops 340475904 | bytes 2065152 | tf_op jit(solution)/shard_map/ic,wcd->wid/dot_general | solution.py:27
  6.3 4.5 %collective-permute-start = (bf16[3,384,384]{1,2,0:T(8,128)(2,1)}, bf16[3,384,384]{1,2,0:T(8,128)(2,1)}, u32[]{:S(2)}, u32[]{:S(2)}) collective-permute-start(bf16[3,384,384]{1,2,0:T(8,128)(2,1)} %fusion.12), channel_id=1, source_target_pairs={{0,1},{1,2},{2,3},{3,4},{4,5},{5,6},{6,7},{7,8},{8,9},{9,10},{10,1... | collective-permute-start | bytes 2654216 | tf_op jit(solution)/shard_map/ppermute | solution.py:14
  10.8 3.0 %fusion.13 = bf16[3,384,384]{1,2,0:T(8,128)(2,1)} fusion(bf16[1,16,384,384]{3,2,1,0:T(8,128)(2,1)} %param.7, bf16[1,384,384]{2,1,0:T(8,128)(2,1)} %param.5, pred[384]{0:T(512)(128)(4,1)S(1)} %get-tuple-element.11, pred[384]{0:T(512)(128)(4,1)S(1)} %get-tuple-element.12), kind=kOutput, calls=%fused_computation.23 | convolution fusion | flops 340475904 | bytes 2065152 | tf_op jit(solution)/shard_map/ic,wcd->wid/dot_general | solution.py:27
  13.8 1.9 collective-permute-start.1
  15.7 0.0 copy-done
  15.7 2.9 %fusion.14 = bf16[3,384,384]{1,2,0:T(8,128)(2,1)} fusion(bf16[1,16,384,384]{3,2,1,0:T(8,128)(2,1)} %param.7, bf16[1,384,384]{2,1,0:T(8,128)(2,1)S(1)} %copy-done, pred[384]{0:T(512)(128)(4,1)S(1)} %get-tuple-element.11, pred[384]{0:T(512)(128)(4,1)S(1)} %get-tuple-element.12), kind=kOutput, calls=%fused_computation.24 | convolution fusion | flops 340475904 | bytes 2065152 | tf_op jit(solution)/shard_map/ic,wcd->wid/dot_general | solution.py:27
  18.6 4.3 %collective-permute-start.2 = (bf16[3,384,384]{1,2,0:T(8,128)(2,1)}, bf16[3,384,384]{1,2,0:T(8,128)(2,1)S(1)}, u32[]{:S(2)}, u32[]{:S(2)}) collective-permute-start(bf16[3,384,384]{1,2,0:T(8,128)(2,1)} %fusion.14), channel_id=1, source_target_pairs={{0,8},{1,9},{2,10},{3,11},{4,12},{5,13},{6,14},{7,15},{16,24},{17,... | collective-permute-start | bytes 2654216 | tf_op jit(solution)/shard_map/ppermute | solution.py:14
  22.9 2.9 %fusion.15 = bf16[3,384,384]{1,2,0:T(8,128)(2,1)} fusion(bf16[1,16,384,384]{3,2,1,0:T(8,128)(2,1)} %param.7, bf16[1,384,384]{2,1,0:T(8,128)(2,1)S(1)} %copy-done, pred[384]{0:T(512)(128)(4,1)S(1)} %get-tuple-element.11, pred[384]{0:T(512)(128)(4,1)S(1)} %get-tuple-element.12), kind=kOutput, calls=%fused_computation.25 | convolution fusion | flops 340475904 | bytes 2065152 | tf_op jit(solution)/shard_map/ic,wcd->wid/dot_general | solution.py:27
  25.8 1.3 collective-permute-start.3
  27.1 0.2 copy.7
  27.3 2.3 %fusion.9 = bf16[16,384,384]{1,2,0:T(8,128)(2,1)S(1)} fusion(bf16[1,16,384,384]{3,2,1,0:T(8,128)(2,1)} %param.7, bf16[1,384,384]{2,1,0:T(8,128)(2,1)S(1)} %copy-done, pred[384]{0:T(512)(128)(4,1)S(1)} %get-tuple-element.11, pred[384]{0:T(512)(128)(4,1)S(1)} %get-tuple-element.12), kind=kOutput, calls=%fused_computation.19 | convolution fusion | flops 453869568 | bytes 2654976 | tf_op jit(solution)/shard_map/ic,wcd->wid/dot_general | solution.py:27
  29.6 1.0 collective-permute-done
  30.6 1.3 constant_dynamic-update-slice_fusion.3
  31.9 0.0 collective-permute-done.1
  31.9 0.2 constant_dynamic-update-slice_fusion.2
  32.1 8.5 %collective-permute-done.2 = bf16[3,384,384]{1,2,0:T(8,128)(2,1)S(1)} collective-permute-done((bf16[3,384,384]{1,2,0:T(8,128)(2,1)}, bf16[3,384,384]{1,2,0:T(8,128)(2,1)S(1)}, u32[]{:S(2)}, u32[]{:S(2)}) %collective-permute-start.2) | collective-permute-done | bytes 884768 | tf_op jit(solution)/shard_map/ppermute | solution.py:14
  40.6 0.2 constant_dynamic-update-slice_fusion.1
  40.8 27.4 %collective-permute-done.3 = bf16[3,384,384]{1,2,0:T(8,128)(2,1)S(1)} collective-permute-done((bf16[3,384,384]{1,2,0:T(8,128)(2,1)}, bf16[3,384,384]{1,2,0:T(8,128)(2,1)S(1)}, u32[]{:S(2)}, u32[]{:S(2)}) %collective-permute-start.3) | collective-permute-done | bytes 884768 | tf_op jit(solution)/shard_map/ppermute | solution.py:14
  68.2 0.2 constant_dynamic-update-slice_fusion
  68.4 5.7 %fusion.76 = (f32[]{:T(128)}, f32[]{:T(128)}, bf16[384,384]{0,1:T(8,128)(2,1)S(1)}) fusion(bf16[1,384,384]{1,2,0:T(8,128)(2,1)S(1)} %copy.7, pred[384]{0:T(512)(128)(4,1)S(1)} %get-tuple-element.11, pred[384]{0:T(512)(128)(4,1)S(1)} %get-tuple-element.12, bf16[1,16,384,384]{3,2,1,0:T(8,128)(2,1)} %param.6, ...), kind=kOutput, calls=%fused_computation.63 | convolution fusion | flops 1815773184 | bytes 10027816 | tf_op jit(solution)/shard_map/wij,wjd->id/dot_general | solution.py:39
  74.0 31.0 %all-reduce = (f32[]{:T(128)}, f32[]{:T(128)}) all-reduce(f32[]{:T(128)} %get-tuple-element.5, f32[]{:T(128)} %get-tuple-element.4), channel_id=1, replica_groups=mesh['rep'=2,'sec'=16] {'sec'}, use_global_device_ids=true, to_apply=%region_1.2 | all-reduce | flops 2 | bytes 16 | tf_op jit(solution)/shard_map/psum | solution.py:56
  106.4 0.9 multiply_reduce_fusion
  107.3 30.1 %psum.23 = f32[]{:T(128)} all-reduce(f32[]{:T(128)} %multiply_reduce_fusion), channel_id=1, replica_groups=mesh['rep'=2,'sec'=16] {'sec'}, use_global_device_ids=true, to_apply=%region_5.6 | all-reduce | flops 1 | bytes 8 | tf_op jit(solution)/shard_map/psum | solution.py:61
  138.1 0.2 fusion.78
  138.4 2.9 %fusion.16 = bf16[3,384,384]{1,2,0:T(8,128)(2,1)} fusion(bf16[384,384,1]{0,1,2:T(8,128)(2,1)S(1)} %fusion.78, bf16[1,16,384,384]{3,2,1,0:T(8,128)(2,1)} %param.7), kind=kOutput, calls=%fused_computation.26 | convolution fusion | flops 340180992 | bytes 2064384 | tf_op jit(solution)/shard_map/ic,wcd->wid/dot_general | solution.py:27
  141.2 2.8 %fusion.17 = bf16[3,384,384]{1,2,0:T(8,128)(2,1)} fusion(bf16[384,384,1]{0,1,2:T(8,128)(2,1)S(1)} %fusion.78, bf16[1,16,384,384]{3,2,1,0:T(8,128)(2,1)} %param.7), kind=kOutput, calls=%fused_computation.27 | convolution fusion | flops 340180992 | bytes 2064384 | tf_op jit(solution)/shard_map/ic,wcd->wid/dot_general | solution.py:27
  144.1 1.9 collective-permute-start.4
  146.0 2.8 %fusion.18 = bf16[3,384,384]{1,2,0:T(8,128)(2,1)} fusion(bf16[384,384,1]{0,1,2:T(8,128)(2,1)S(1)} %fusion.78, bf16[1,16,384,384]{3,2,1,0:T(8,128)(2,1)} %param.7), kind=kOutput, calls=%fused_computation.28 | convolution fusion | flops 340180992 | bytes 2064384 | tf_op jit(solution)/shard_map/ic,wcd->wid/dot_general | solution.py:27
  148.8 3.3 %collective-permute-start.5 = (bf16[3,384,384]{1,2,0:T(8,128)(2,1)}, bf16[3,384,384]{1,2,0:T(8,128)(2,1)S(1)}, u32[]{:S(2)}, u32[]{:S(2)}) collective-permute-start(bf16[3,384,384]{1,2,0:T(8,128)(2,1)} %fusion.17), channel_id=1, source_target_pairs={{1,0},{2,1},{3,2},{4,3},{5,4},{6,5},{7,6},{8,7},{9,8},{10,9},{11,1... | collective-permute-start | bytes 2654216 | tf_op jit(solution)/shard_map/ppermute | solution.py:14
  152.2 1.3 collective-permute-start.6
  153.5 2.9 %fusion.19 = bf16[3,384,384]{1,2,0:T(8,128)(2,1)} fusion(bf16[384,384,1]{0,1,2:T(8,128)(2,1)S(1)} %fusion.78, bf16[1,16,384,384]{3,2,1,0:T(8,128)(2,1)} %param.7), kind=kOutput, calls=%fused_computation.29 | convolution fusion | flops 340180992 | bytes 2064384 | tf_op jit(solution)/shard_map/ic,wcd->wid/dot_general | solution.py:27
  156.4 1.5 collective-permute-start.7
  157.8 0.9 copy.8
  158.7 2.2 %fusion.11 = bf16[16,384,384]{1,2,0:T(8,128)(2,1)S(1)} fusion(bf16[384,384,1]{0,1,2:T(8,128)(2,1)S(1)} %fusion.78, bf16[1,16,384,384]{3,2,1,0:T(8,128)(2,1)} %param.7), kind=kOutput, calls=%fused_computation.21 | convolution fusion | flops 453574656 | bytes 2654208 | tf_op jit(solution)/shard_map/ic,wcd->wid/dot_general | solution.py:27
  160.9 4.8 %collective-permute-done.4 = bf16[3,384,384]{1,2,0:T(8,128)(2,1)} collective-permute-done((bf16[3,384,384]{1,2,0:T(8,128)(2,1)}, bf16[3,384,384]{1,2,0:T(8,128)(2,1)}, u32[]{:S(2)}, u32[]{:S(2)}) %collective-permute-start.4) | collective-permute-done | bytes 884768 | tf_op jit(solution)/shard_map/ppermute | solution.py:14
  165.8 1.3 constant_dynamic-update-slice_fusion.7
  167.1 0.0 collective-permute-done.5
  167.1 0.2 constant_dynamic-update-slice_fusion.6
  167.3 5.5 %collective-permute-done.6 = bf16[3,384,384]{1,2,0:T(8,128)(2,1)S(1)} collective-permute-done((bf16[3,384,384]{1,2,0:T(8,128)(2,1)}, bf16[3,384,384]{1,2,0:T(8,128)(2,1)S(1)}, u32[]{:S(2)}, u32[]{:S(2)}) %collective-permute-start.6) | collective-permute-done | bytes 884768 | tf_op jit(solution)/shard_map/ppermute | solution.py:14
  172.8 0.2 constant_dynamic-update-slice_fusion.5
  173.0 25.1 %collective-permute-done.7 = bf16[3,384,384]{1,2,0:T(8,128)(2,1)S(1)} collective-permute-done((bf16[3,384,384]{1,2,0:T(8,128)(2,1)}, bf16[3,384,384]{1,2,0:T(8,128)(2,1)S(1)}, u32[]{:S(2)}, u32[]{:S(2)}) %collective-permute-start.7) | collective-permute-done | bytes 884768 | tf_op jit(solution)/shard_map/ppermute | solution.py:14
  198.1 0.2 constant_dynamic-update-slice_fusion.4
  198.3 5.0 %fusion.52 = bf16[1,384,384]{1,2,0:T(8,128)(2,1)S(1)} fusion(bf16[1,16,384,384]{3,2,1,0:T(8,128)(2,1)} %param.6, bf16[16,384,384]{1,2,0:T(8,128)(2,1)S(1)} %constant_dynamic-update-slice_fusion.4, bf16[16]{0:T(256)(128)(2,1)S(1)} %convert_bitcast_fusion, pred[384]{0:T(512)(128)(4,1)S(1)} %get-tuple-element.12, pred[384]{0:T(512)(128)(4,1)S(1)} %get-tuple-element.11), kind=kOutput, calls=%fused_computation.38 | convolution fusion | flops 1814740992 | bytes 9732896 | tf_op jit(solution)/shard_map/wij,wjd->id/dot_general | solution.py:39
  203.3 0.9 copy.9
  (2 shorter events, 0.0 us)
Async XLA Ops:
  0.6 15.1 %copy-start = (bf16[1,384,384]{2,1,0:T(8,128)(2,1)S(1)}, bf16[1,384,384]{2,1,0:T(8,128)(2,1)}, u32[]{:S(2)}) copy-start(bf16[1,384,384]{2,1,0:T(8,128)(2,1)} %param.5) | copy-start | bytes 884740
  3.3 24.0 %copy-start.1 = (s32[1,16]{1,0:T(1,128)S(1)}, s32[1,16]{1,0:T(1,128)}, u32[]{:S(2)}) copy-start(s32[1,16]{1,0:T(1,128)} %param.9) | copy-start | bytes 196
  6.3 24.3 %collective-permute-start = (bf16[3,384,384]{1,2,0:T(8,128)(2,1)}, bf16[3,384,384]{1,2,0:T(8,128)(2,1)}, u32[]{:S(2)}, u32[]{:S(2)}) collective-permute-start(bf16[3,384,384]{1,2,0:T(8,128)(2,1)} %fusion.12), channel_id=1, source_target_pairs={{0,1},{1,2},{2,3},{3,4},{4,5},{5,6},{6,7},{7,8},{8,9},{9,10},{10,1... | collective-permute-start | bytes 2654216 | tf_op jit(solution)/shard_map/ppermute | solution.py:14
  13.8 18.1 %collective-permute-start.1 = (bf16[3,384,384]{1,2,0:T(8,128)(2,1)}, bf16[3,384,384]{1,2,0:T(8,128)(2,1)S(1)}, u32[]{:S(2)}, u32[]{:S(2)}) collective-permute-start(bf16[3,384,384]{1,2,0:T(8,128)(2,1)} %fusion.13), channel_id=1, source_target_pairs={{1,0},{2,1},{3,2},{4,3},{5,4},{6,5},{7,6},{8,7},{9,8},{10,9},{11,1... | collective-permute-start | bytes 2654216 | tf_op jit(solution)/shard_map/ppermute | solution.py:14
  18.6 22.0 %collective-permute-start.2 = (bf16[3,384,384]{1,2,0:T(8,128)(2,1)}, bf16[3,384,384]{1,2,0:T(8,128)(2,1)S(1)}, u32[]{:S(2)}, u32[]{:S(2)}) collective-permute-start(bf16[3,384,384]{1,2,0:T(8,128)(2,1)} %fusion.14), channel_id=1, source_target_pairs={{0,8},{1,9},{2,10},{3,11},{4,12},{5,13},{6,14},{7,15},{16,24},{17,... | collective-permute-start | bytes 2654216 | tf_op jit(solution)/shard_map/ppermute | solution.py:14
  25.8 42.4 %collective-permute-start.3 = (bf16[3,384,384]{1,2,0:T(8,128)(2,1)}, bf16[3,384,384]{1,2,0:T(8,128)(2,1)S(1)}, u32[]{:S(2)}, u32[]{:S(2)}) collective-permute-start(bf16[3,384,384]{1,2,0:T(8,128)(2,1)} %fusion.15), channel_id=1, source_target_pairs={{8,0},{9,1},{10,2},{11,3},{12,4},{13,5},{14,6},{15,7},{24,16},{25,... | collective-permute-start | bytes 2654216 | tf_op jit(solution)/shard_map/ppermute | solution.py:14
  144.1 21.7 %collective-permute-start.4 = (bf16[3,384,384]{1,2,0:T(8,128)(2,1)}, bf16[3,384,384]{1,2,0:T(8,128)(2,1)}, u32[]{:S(2)}, u32[]{:S(2)}) collective-permute-start(bf16[3,384,384]{1,2,0:T(8,128)(2,1)} %fusion.16), channel_id=1, source_target_pairs={{0,1},{1,2},{2,3},{3,4},{4,5},{5,6},{6,7},{7,8},{8,9},{9,10},{10,1... | collective-permute-start | bytes 2654216 | tf_op jit(solution)/shard_map/ppermute | solution.py:14
  148.8 18.3 %collective-permute-start.5 = (bf16[3,384,384]{1,2,0:T(8,128)(2,1)}, bf16[3,384,384]{1,2,0:T(8,128)(2,1)S(1)}, u32[]{:S(2)}, u32[]{:S(2)}) collective-permute-start(bf16[3,384,384]{1,2,0:T(8,128)(2,1)} %fusion.17), channel_id=1, source_target_pairs={{1,0},{2,1},{3,2},{4,3},{5,4},{6,5},{7,6},{8,7},{9,8},{10,9},{11,1... | collective-permute-start | bytes 2654216 | tf_op jit(solution)/shard_map/ppermute | solution.py:14
  152.2 20.7 %collective-permute-start.6 = (bf16[3,384,384]{1,2,0:T(8,128)(2,1)}, bf16[3,384,384]{1,2,0:T(8,128)(2,1)S(1)}, u32[]{:S(2)}, u32[]{:S(2)}) collective-permute-start(bf16[3,384,384]{1,2,0:T(8,128)(2,1)} %fusion.18), channel_id=1, source_target_pairs={{0,8},{1,9},{2,10},{3,11},{4,12},{5,13},{6,14},{7,15},{16,24},{17,... | collective-permute-start | bytes 2654216 | tf_op jit(solution)/shard_map/ppermute | solution.py:14
  156.4 41.7 %collective-permute-start.7 = (bf16[3,384,384]{1,2,0:T(8,128)(2,1)}, bf16[3,384,384]{1,2,0:T(8,128)(2,1)S(1)}, u32[]{:S(2)}, u32[]{:S(2)}) collective-permute-start(bf16[3,384,384]{1,2,0:T(8,128)(2,1)} %fusion.19), channel_id=1, source_target_pairs={{8,0},{9,1},{10,2},{11,3},{12,4},{13,5},{14,6},{15,7},{24,16},{25,... | collective-permute-start | bytes 2654216 | tf_op jit(solution)/shard_map/ppermute | solution.py:14
where the time goes:
time: 205 us; the launch traced here: 204 us
  waiting for transfers between devices  72.4 us (35%)
  blocking collectives  61.1 us (30%)
  matrix products  38.3 us (19%)
  starting transfers between devices  20 us (10%)
  local copies, waits for them, and re-layouts  7.05 us (3%)
  between operations  2.83 us (1%)
  other arithmetic  2.47 us (1%)
    ppermute x8, waiting for transfers between devices, shifted(): return lax.ppermute(value, axis, pairs)  72.4 us
    psum x1, blocking collectives, on_device(): lax.psum((jnp.sum(first_values * applied_values), jnp.sum(first_values *...  31 us
    psum x1, blocking collectives, on_device(): spread = lax.psum(jnp.sum(residual * residual), 'sec')  30.1 us
    dot_general x10, matrix products, times_maps(): jnp.einsum('ic,wcd->wid', vector, right_maps, preferred_element_type=jnp....  27.6 us
    ppermute x8, starting transfers between devices, shifted(): return lax.ppermute(value, axis, pairs)  20 us
    dot_general x2, matrix products, apply_hamiltonian(): jnp.einsum('wij,wjd->id', left_blocks, stacked, preferred_element_type=jn...  10.6 us
    unnamed x13, local copies, waits for them, and re-layouts  5.4 us
  transfers between devices with their start and end apart: 8, of which 6 were waited for; matrix products, arithmetic and copies ran while one was open for 11% of the time, Pallas kernels for 0%

commit v1 on v0

v1 whole, which is shorter than its diff:
```python
import functools

import jax
import jax.numpy as jnp
from jax import lax
from jax.experimental import pallas as pl
from jax.experimental.pallas import tpu as pltpu
from jax.sharding import PartitionSpec as P

ONSITE = 4
HOPS = 3
ND = 8
F32 = jnp.float32
BF16 = jnp.bfloat16


def hop_slots(me, sectors):
    down = lax.rem(me, ND)
    base = [ONSITE + HOPS * i for i in range(4)]
    slots = [
        (me - 1, down > 0, me + 1, (down < ND - 1) & (me + 1 < sectors), base[0], base[0]),
        (me + 1, (down < ND - 1) & (me + 1 < sectors), me - 1, down > 0, base[1], base[1]),
    ]
    if sectors == 2 * ND:
        high = me >= ND
        partner = lax.rem(me + ND, sectors)
        slots.append(
            (partner, None, partner, None, jnp.where(high, base[2], base[3]), jnp.where(high, base[3], base[2]))
        )
    else:
        slots.append((me - ND, me >= ND, me + ND, me + ND < sectors, base[2], base[2]))
        slots.append((me + ND, me + ND < sectors, me - ND, me >= ND, base[3], base[3]))
    return slots


def when(condition):
    if condition is None:
        return lambda f: f()
    return pl.when(condition)


def kernel(
    sectors, chunks, sizes_ref, links_ref, wave_hbm, left_hbm, right_hbm,
    first_out, second_out,
    wave, vec, left, right_on, right_hop0, right_hop1, vec_hop, app_hop0, app_hop1, acc_ref, stat_src, stats,
    local_sem, right_send, right_recv, vec_send, vec_recv, app_send, app_recv, stat_send, stat_recv,
):
    me = lax.axis_index("sec")
    block = wave.shape[0]
    slots = hop_slots(me, sectors)
    right_hop = (right_hop0, right_hop1)
    app_hop = (app_hop0, app_hop1)

    load_wave = pltpu.make_async_copy(wave_hbm.at[0], wave, local_sem.at[0])
    load_on = pltpu.make_async_copy(right_hbm.at[0, pl.ds(0, ONSITE)], right_on, local_sem.at[1])
    load_left = pltpu.make_async_copy(left_hbm.at[0], left, local_sem.at[2])
    load_wave.start()
    load_on.start()
    load_left.start()

    barrier = pltpu.get_barrier_semaphore()

    @pl.loop(1, sectors)
    def _(i):
        pl.semaphore_signal(
            barrier, inc=1, device_id={"sec": lax.rem(me + i, sectors)}, device_id_type=pl.DeviceIdType.MESH
        )

    pl.semaphore_wait(barrier, sectors - 1)

    def remote(src, dst, send, recv, device):
        return pltpu.make_async_remote_copy(
            src_ref=src, dst_ref=dst, send_sem=send, recv_sem=recv,
            device_id={"sec": device}, device_id_type=pl.DeviceIdType.MESH,
        )

    def right_copy(s, c):
        start, width = chunks[c]
        return remote(
            right_hbm.at[0, pl.ds(slots[s][5], HOPS), :, pl.ds(start, width)],
            right_hop[c].at[s], right_send.at[s, c], right_recv.at[s, c], slots[s][2],
        )

    def vec_copy(s):
        return remote(vec, vec_hop.at[s], vec_send.at[s], vec_recv.at[s], slots[s][2])

    def app_copy(s, c):
        start, width = chunks[c]
        return remote(
            first_out.at[0, :, pl.ds(start, width)],
            app_hop[c].at[s], app_send.at[s, c], app_recv.at[s, c], slots[s][2],
        )

    order = list(range(len(slots)))[::-1]
    for s in order:
        when(slots[s][3])(lambda s=s: right_copy(s, 0).start())

    load_wave.wait()
    rows_live = sizes_ref[0, 0]
    cols_live = sizes_ref[0, 1]
    row_at = lax.broadcasted_iota(jnp.int32, (block, block), 0)
    col_at = lax.broadcasted_iota(jnp.int32, (block, block), 1)
    live = (row_at < rows_live) & (col_at < cols_live)
    vec[...] = jnp.where(live, wave[...].astype(F32), 0.0).astype(BF16)
    for s in order:
        when(slots[s][3])(lambda s=s: vec_copy(s).start())
    load_on.wait()
    load_left.wait()

    def terms(vector, rights, base, count):
        total = None
        for j in range(count):
            product = jnp.dot(vector, rights(j), preferred_element_type=F32)
            product = (product * links_ref[0, base + j].astype(F32)).astype(BF16)
            part = jnp.dot(left[base + j], product, preferred_element_type=F32)
            total = part if total is None else total + part
        return total

    def onsite(vector_ref, c):
        start, width = chunks[c]
        cols = pl.ds(start, width)
        acc_ref[:, cols] = terms(vector_ref[...], lambda j: right_on[j, :, cols], 0, ONSITE)

    def hop(s, c):
        start, width = chunks[c]
        acc_ref[:, pl.ds(start, width)] += terms(vec_hop[s], lambda j: right_hop[c][s, j], slots[s][4], HOPS)

    def finish(out_ref, c):
        start, width = chunks[c]
        cols = pl.ds(start, width)
        rows = lax.broadcasted_iota(jnp.int32, (block, width), 0)
        at = lax.broadcasted_iota(jnp.int32, (block, width), 1) + start
        region = (rows < rows_live) & (at < cols_live)
        out_ref[0, :, cols] = jnp.where(region, acc_ref[:, cols], 0.0).astype(BF16)

    count = len(slots)
    for c in range(2):
        onsite(vec, c)
    for s in order:
        def next_chunk(s=s):
            right_copy(s, 0).wait_send()
            right_copy(s, 1).start()

        when(slots[s][3])(next_chunk)
    for c in range(2):
        for s in range(count):
            def arrived(s=s, c=c):
                if c == 0:
                    vec_copy(s).wait_recv()
                right_copy(s, c).wait_recv()
                hop(s, c)

            when(slots[s][1])(arrived)
        finish(first_out, c)
        for s in order:
            when(slots[s][3])(lambda s=s, c=c: app_copy(s, c).start())

    v = vec[...].astype(F32)
    a = first_out[0].astype(F32)
    corr = jnp.sum(v * a)
    norm = jnp.sum(v * v)
    local = jnp.full((1, 1), corr, F32) / (jnp.full((1, 1), norm, F32) + 1e-06)
    off = a - local * v
    square = jnp.sum(off * off)
    cross = jnp.sum(off * v)
    row = lax.broadcasted_iota(jnp.int32, (8, 128), 0)
    tile = jnp.where(row == 0, corr, jnp.where(row == 1, norm, jnp.where(row == 2, square, cross)))
    stat_src[...] = jnp.where(row == 4, jnp.broadcast_to(local, (8, 128)), tile)
    stats[me] = stat_src[...]

    def stat_copy(peer, slot):
        return remote(stat_src, stats.at[slot], stat_send.at[peer], stat_recv.at[slot], peer)

    @pl.loop(1, sectors)
    def _(i):
        stat_copy(lax.rem(me + i, sectors), me).start()

    @pl.loop(1, sectors)
    def _(i):
        peer = lax.rem(me + i, sectors)
        stat_copy(peer, peer).wait_recv()

    def column(i):
        return stats[:, i : i + 1, :]

    corr_all = jnp.sum(column(0), axis=0)
    norm_all = jnp.sum(column(1), axis=0)
    ray = corr_all / (norm_all + 1e-06)
    gap = ray[None] - column(4)
    spread = jnp.sum(column(2) - 2.0 * gap * column(3) + gap * gap * column(1), axis=0)
    scale = lax.rsqrt(jnp.maximum(spread, 0.0) / float(sectors * block * block) + 1e-06)
    ray = ray[:, 0:1]
    scale = scale[:, 0:1]

    wave[...] = ((a - ray * v) * scale).astype(BF16)
    for c in range(2):
        onsite(wave, c)
    for s in range(count):
        def again(s=s):
            for c in range(2):
                start, width = chunks[c]
                cols = pl.ds(start, width)
                app_copy(s, c).wait_recv()
                before = vec_hop[s, :, cols].astype(F32)
                vec_hop[s, :, cols] = ((app_hop[c][s].astype(F32) - ray * before) * scale).astype(BF16)
            for c in range(2):
                hop(s, c)

        when(slots[s][1])(again)
    for c in range(2):
        finish(second_out, c)

    for s in order:
        def drain(s=s):
            vec_copy(s).wait_send()
            right_copy(s, 1).wait_send()
            for c in range(2):
                app_copy(s, c).wait_send()

        when(slots[s][3])(drain)

    @pl.loop(1, sectors)
    def _(i):
        stat_copy(lax.rem(me + i, sectors), me).wait_send()


def on_device(sectors, wavefunction, left_env, right_env, sector_sizes, term_links):
    block = wavefunction.shape[1]
    terms = left_env.shape[1]
    split = 256 if block > 256 else block // 2
    chunks = ((0, split), (split, block - split))
    count = 3 if sectors == 2 * ND else 4
    dma = pltpu.SemaphoreType.DMA
    return pl.pallas_call(
        functools.partial(kernel, sectors, chunks),
        out_shape=(jax.ShapeDtypeStruct((1, block, block), BF16),) * 2,
        in_specs=[pl.BlockSpec(memory_space=pltpu.SMEM)] * 2 + [pl.BlockSpec(memory_space=pl.ANY)] * 3,
        out_specs=(pl.BlockSpec(memory_space=pltpu.VMEM),) * 2,
        scratch_shapes=[
            pltpu.VMEM((block, block), BF16),
            pltpu.VMEM((block, block), BF16),
            pltpu.VMEM((terms, block, block), BF16),
            pltpu.VMEM((ONSITE, block, block), BF16),
            pltpu.VMEM((count, HOPS, block, chunks[0][1]), BF16),
            pltpu.VMEM((count, HOPS, block, chunks[1][1]), BF16),
            pltpu.VMEM((count, block, block), BF16),
            pltpu.VMEM((count, block, chunks[0][1]), BF16),
            pltpu.VMEM((count, block, chunks[1][1]), BF16),
            pltpu.VMEM((block, block), F32),
            pltpu.VMEM((8, 128), F32),
            pltpu.VMEM((sectors, 8, 128), F32),
            dma((3,)),
            dma((count, 2)),
            dma((count, 2)),
            dma((count,)),
            dma((count,)),
            dma((count, 2)),
            dma((count, 2)),
            dma((sectors,)),
            dma((sectors,)),
        ],
        compiler_params=pltpu.CompilerParams(
            collective_id=0, has_side_effects=True, vmem_limit_bytes=40 * 1024 * 1024
        ),
        cost_estimate=pl.CostEstimate(
            flops=8 * terms * block**3, bytes_accessed=4 * terms * block * block, transcendentals=0
        ),
    )(sector_sizes, term_links, wavefunction, left_env, right_env)


def solution(mesh):
    return jax.shard_map(
        functools.partial(on_device, mesh.shape["sec"]),
        mesh=mesh,
        in_specs=(
            P(("rep", "sec"), None, None),
            P(("rep", "sec"), None, None, None),
            P(("rep", "sec"), None, None, None),
            P("sec", None),
            P("sec", None),
        ),
        out_specs=(P(("rep", "sec"), None, None), P(("rep", "sec"), None, None)),
        check_vma=False,
    )
```

time: 205 us -> 89.6 us (0.44)
  Pallas kernels: 0 us -> 80.3 us
  waiting for transfers between devices: 72.4 us -> 0 us
  blocking collectives: 61.1 us -> 0 us
  matrix products: 38.3 us -> 0 us
  starting transfers between devices: 20 us -> 0 us
  other arithmetic: 2.47 us -> 0 us
  between operations: 2.83 us -> 0.65 us
    pallas_call x0 -> x1, Pallas kernels: none -> 80.3 us  [on_device(): pl.pallas_call(functools.partial(kernel, sectors, chunks), out_shape=(jax...]
    ppermute x8 -> x0, waiting for transfers between devices: 72.4 us -> none  [shifted(): return lax.ppermute(value, axis, pairs)]
    psum x2 -> x0, blocking collectives: 61.1 us -> none  [the longest x1 31 us: on_device(): lax.psum((jnp.sum(first_values * applied_values), jnp.sum(first_values *...]
    dot_general x12 -> x0, matrix products: 38.3 us -> none  [the longest x10 27.6 us: times_maps(): jnp.einsum('ic,wcd->wid', vector, right_maps, preferred_element_type=jnp....]
    ppermute x8 -> x0, starting transfers between devices: 20 us -> none  [shifted(): return lax.ppermute(value, axis, pairs)]
    unnamed x13 -> x12, local copies, waits for them, and re-layouts: 5.4 us -> 8.37 us
  transfers between devices with their start and end apart: 8 -> 0, of which waited for: 6 -> 0; matrix products, arithmetic and copies ran while one was open for 11% -> 0% of each run, Pallas kernels for 0% -> 0%
where the time goes in v1:
time: 89.6 us; the launch traced here: 89.3 us
  Pallas kernels  80.3 us (90%)
  local copies, waits for them, and re-layouts  8.37 us (9%)
    pallas_call x1, Pallas kernels, on_device(): pl.pallas_call(functools.partial(kernel, sectors, chunks), out_shape=(jax...  80.3 us
    unnamed x12, local copies, waits for them, and re-layouts  8.37 us

profile of v1, /device:TPU:1, one launch (start us, length us, event | category | flops | bytes accessed | tf_op | source)
XLA Modules:
  0.0 89.3 jit_solution(11581186142407456111)
XLA Ops:
  0.6 0.0 copy-start
  0.6 2.3 %copy-done = bf16[1,16,384,384]{3,2,1,0:T(8,128)(2,1)S(1)} copy-done((bf16[1,16,384,384]{3,2,1,0:T(8,128)(2,1)S(1)}, bf16[1,16,384,384]{3,2,1,0:T(8,128)(2,1)}, u32[]{:S(2)}) %copy-start) | copy-done | bytes 4718616
  3.0 0.0 copy-start.1
  3.0 2.3 %copy-done.1 = bf16[1,16,384,384]{3,2,1,0:T(8,128)(2,1)S(1)} copy-done((bf16[1,16,384,384]{3,2,1,0:T(8,128)(2,1)S(1)}, bf16[1,16,384,384]{3,2,1,0:T(8,128)(2,1)}, u32[]{:S(2)}) %copy-start.1) | copy-done | bytes 4718616
  5.3 0.0 copy-start.2
  5.3 1.0 %copy-done.2 = bf16[1,384,384]{2,1,0:T(8,128)(2,1)S(1)} copy-done((bf16[1,384,384]{2,1,0:T(8,128)(2,1)S(1)}, bf16[1,384,384]{2,1,0:T(8,128)(2,1)}, u32[]{:S(2)}) %copy-start.2) | copy-done | bytes 294936
  6.3 0.0 copy-start.3
  6.3 0.7 copy-done.3
  6.9 0.0 copy-start.4
  6.9 0.7 copy-done.4
  7.6 80.3 %shard_map.68 = (bf16[1,384,384]{2,1,0:T(8,128)(2,1)S(1)}, bf16[1,384,384]{2,1,0:T(8,128)(2,1)S(1)}) custom-call(s32[1,2]{1,0:T(1,128)S(1)} %copy-done.3, s32[1,16]{1,0:T(1,128)S(1)} %copy-done.4, bf16[1,384,384]{2,1,0:T(8,128)(2,1)S(1)} %copy-done.2, bf16[1,16,384,384]{3,2,1,0:T(8,128)(2,1)S(1)} %copy-done, bf16[1,16,384,384]{3,2,1,0:T(8,128)(2,1)S(1)} %copy-done.1), custom_call_target="tpu_custom_call" | custom-call | flops 7247757312 | bytes 9437184 | tf_op jit(solution)/shard_map/pallas_call | solution.py:234
  87.9 0.7 copy.9
  88.6 0.7 copy.10
Async XLA Ops:
  0.6 2.3 %copy-start = (bf16[1,16,384,384]{3,2,1,0:T(8,128)(2,1)S(1)}, bf16[1,16,384,384]{3,2,1,0:T(8,128)(2,1)}, u32[]{:S(2)}) copy-start(bf16[1,16,384,384]{3,2,1,0:T(8,128)(2,1)} %left_hbm.1) | copy-start | bytes 14155780
  3.0 2.3 %copy-start.1 = (bf16[1,16,384,384]{3,2,1,0:T(8,128)(2,1)S(1)}, bf16[1,16,384,384]{3,2,1,0:T(8,128)(2,1)}, u32[]{:S(2)}) copy-start(bf16[1,16,384,384]{3,2,1,0:T(8,128)(2,1)} %right_hbm.1) | copy-start | bytes 14155780
  5.3 1.0 %copy-start.2 = (bf16[1,384,384]{2,1,0:T(8,128)(2,1)S(1)}, bf16[1,384,384]{2,1,0:T(8,128)(2,1)}, u32[]{:S(2)}) copy-start(bf16[1,384,384]{2,1,0:T(8,128)(2,1)} %wave_hbm.1) | copy-start | bytes 884740
  6.3 0.7 copy-start.3
  6.9 0.7 copy-start.4

commit v2 on v1

--- a/solution.py
+++ b/solution.py
@@ -40,10 +40,10 @@
 
 
 def kernel(
-    sectors, chunks, sizes_ref, links_ref, wave_hbm, left_hbm, right_hbm,
+    sectors, chunks, sizes_hbm, links_hbm, wave_hbm, left_hbm, right_hbm,
     first_out, second_out,
-    wave, vec, left, right_on, right_hop0, right_hop1, vec_hop, app_hop0, app_hop1, acc_ref, stat_src, stats,
-    local_sem, right_send, right_recv, vec_send, vec_recv, app_send, app_recv, stat_send, stat_recv,
+    sizes_ref, links_ref, wave, vec, left, right_on0, right_on1, right_hop0, right_hop1, vec_hop, app_hop0, app_hop1, acc_ref, stat_src, stats,
+    local_sem, left_sem, on_sem, right_send, right_recv, vec_send, vec_recv, app_send, app_recv, stat_send, stat_recv,
 ):
     me = lax.axis_index("sec")
     block = wave.shape[0]
@@ -51,12 +51,28 @@
     right_hop = (right_hop0, right_hop1)
     app_hop = (app_hop0, app_hop1)
 
+    count = len(slots)
+    wide, narrow = chunks[0][1], chunks[1][1]
     load_wave = pltpu.make_async_copy(wave_hbm.at[0], wave, local_sem.at[0])
-    load_on = pltpu.make_async_copy(right_hbm.at[0, pl.ds(0, ONSITE)], right_on, local_sem.at[1])
-    load_left = pltpu.make_async_copy(left_hbm.at[0], left, local_sem.at[2])
+    load_sizes = pltpu.make_async_copy(sizes_hbm, sizes_ref, local_sem.at[1])
+    load_links = pltpu.make_async_copy(links_hbm, links_ref, local_sem.at[2])
     load_wave.start()
-    load_on.start()
-    load_left.start()
+    load_sizes.start()
+    load_links.start()
+    rest = []
+    for w in range(ONSITE):
+        rest.append(
+            pltpu.make_async_copy(right_hbm.at[0, w, :, pl.ds(0, wide)], right_on0.at[w], on_sem.at[0, w])
+        )
+        rest.append(
+            pltpu.make_async_copy(
+                right_hbm.at[0, w, :, pl.ds(wide, narrow)], right_on1.at[:, pl.ds(w * narrow, narrow)], on_sem.at[1, w]
+            )
+        )
+    for w in range(left_hbm.shape[1]):
+        rest.append(
+            pltpu.make_async_copy(left_hbm.at[0, w], left.at[:, pl.ds(w * block, block)], left_sem.at[w])
+        )
 
     barrier = pltpu.get_barrier_semaphore()
 
@@ -74,12 +90,24 @@
             device_id={"sec": device}, device_id_type=pl.DeviceIdType.MESH,
         )
 
-    def right_copy(s, c):
-        start, width = chunks[c]
-        return remote(
-            right_hbm.at[0, pl.ds(slots[s][5], HOPS), :, pl.ds(start, width)],
-            right_hop[c].at[s], right_send.at[s, c], right_recv.at[s, c], slots[s][2],
-        )
+    def right_copies(s, c):
+        start, width = chunks[c]
+        return [
+            remote(
+                right_hbm.at[0, slots[s][5] + j, :, pl.ds(start, width)],
+                right_hop0.at[s, j] if c == 0 else right_hop1.at[s, :, pl.ds(j * width, width)],
+                right_send.at[s, c, j], right_recv.at[s, c, j], slots[s][2],
+            )
+            for j in range(HOPS)
+        ]
+
+    def right_start(s, c):
+        for copy in right_copies(s, c):
+            copy.start()
+
+    def right_sent(s, c):
+        for copy in right_copies(s, c):
+            copy.wait_send()
 
     def vec_copy(s):
         return remote(vec, vec_hop.at[s], vec_send.at[s], vec_recv.at[s], slots[s][2])
@@ -92,10 +120,12 @@
         )
 
     order = list(range(len(slots)))[::-1]
-    for s in order:
-        when(slots[s][3])(lambda s=s: right_copy(s, 0).start())
+    near, far = range(2), range(2, count)
+    for s in far:
+        when(slots[s][3])(lambda s=s: right_start(s, 0))
 
     load_wave.wait()
+    load_sizes.wait()
     rows_live = sizes_ref[0, 0]
     cols_live = sizes_ref[0, 1]
     row_at = lax.broadcasted_iota(jnp.int32, (block, block), 0)
@@ -104,26 +134,38 @@
     vec[...] = jnp.where(live, wave[...].astype(F32), 0.0).astype(BF16)
     for s in order:
         when(slots[s][3])(lambda s=s: vec_copy(s).start())
-    load_on.wait()
-    load_left.wait()
-
-    def terms(vector, rights, base, count):
-        total = None
-        for j in range(count):
-            product = jnp.dot(vector, rights(j), preferred_element_type=F32)
-            product = (product * links_ref[0, base + j].astype(F32)).astype(BF16)
-            part = jnp.dot(left[base + j], product, preferred_element_type=F32)
-            total = part if total is None else total + part
-        return total
+    for s in near:
+        def both(s=s):
+            right_start(s, 0)
+            right_start(s, 1)
+
+        when(slots[s][3])(both)
+    for copy in rest:
+        copy.start()
+    load_links.wait()
+    for copy in rest:
+        copy.wait()
+
+    def terms(vector, rights, base, number, c):
+        if c == 0:
+            raw = [jnp.dot(vector, rights[j], preferred_element_type=F32) for j in range(number)]
+        else:
+            side = jnp.dot(vector, rights[...], preferred_element_type=F32)
+            raw = [side[:, j * narrow : (j + 1) * narrow] for j in range(number)]
+        products = [(raw[j] * links_ref[0, base + j].astype(F32)).astype(BF16) for j in range(number)]
+        at = pl.multiple_of(base * block, 128) if not isinstance(base, int) else base * block
+        return jnp.dot(
+            left[:, pl.ds(at, number * block)], jnp.concatenate(products, axis=0), preferred_element_type=F32
+        )
 
     def onsite(vector_ref, c):
         start, width = chunks[c]
-        cols = pl.ds(start, width)
-        acc_ref[:, cols] = terms(vector_ref[...], lambda j: right_on[j, :, cols], 0, ONSITE)
+        rights = right_on0 if c == 0 else right_on1
+        acc_ref[:, pl.ds(start, width)] = terms(vector_ref[...], rights, 0, ONSITE, c)
 
     def hop(s, c):
         start, width = chunks[c]
-        acc_ref[:, pl.ds(start, width)] += terms(vec_hop[s], lambda j: right_hop[c][s, j], slots[s][4], HOPS)
+        acc_ref[:, pl.ds(start, width)] += terms(vec_hop[s], right_hop[c].at[s], slots[s][4], HOPS, c)
 
     def finish(out_ref, c):
         start, width = chunks[c]
@@ -133,27 +175,41 @@
         region = (rows < rows_live) & (at < cols_live)
         out_ref[0, :, cols] = jnp.where(region, acc_ref[:, cols], 0.0).astype(BF16)
 
-    count = len(slots)
     for c in range(2):
         onsite(vec, c)
-    for s in order:
+    for s in near:
+        def early(s=s):
+            vec_copy(s).wait_recv()
+            for c in range(2):
+                for copy in right_copies(s, c):
+                    copy.wait_recv()
+                hop(s, c)
+
+        when(slots[s][1])(early)
+    for s in far:
         def next_chunk(s=s):
-            right_copy(s, 0).wait_send()
-            right_copy(s, 1).start()
+            right_sent(s, 0)
+            right_start(s, 1)
 
         when(slots[s][3])(next_chunk)
     for c in range(2):
-        for s in range(count):
+        for s in far:
             def arrived(s=s, c=c):
                 if c == 0:
                     vec_copy(s).wait_recv()
-                right_copy(s, c).wait_recv()
+                for copy in right_copies(s, c):
+                    copy.wait_recv()
                 hop(s, c)
 
             when(slots[s][1])(arrived)
         finish(first_out, c)
         for s in order:
-            when(slots[s][3])(lambda s=s, c=c: app_copy(s, c).start())
+            def send(s=s, c=c):
+                if c == 0 and s >= 2:
+                    right_sent(s, 1)
+                app_copy(s, c).start()
+
+            when(slots[s][3])(send)
 
     v = vec[...].astype(F32)
     a = first_out[0].astype(F32)
@@ -213,7 +269,9 @@
     for s in order:
         def drain(s=s):
             vec_copy(s).wait_send()
-            right_copy(s, 1).wait_send()
+            if s < 2:
+                right_sent(s, 0)
+                right_sent(s, 1)
             for c in range(2):
                 app_copy(s, c).wait_send()
 
@@ -234,15 +292,18 @@
     return pl.pallas_call(
         functools.partial(kernel, sectors, chunks),
         out_shape=(jax.ShapeDtypeStruct((1, block, block), BF16),) * 2,
-        in_specs=[pl.BlockSpec(memory_space=pltpu.SMEM)] * 2 + [pl.BlockSpec(memory_space=pl.ANY)] * 3,
+        in_specs=[pl.BlockSpec(memory_space=pltpu.HBM)] * 5,
         out_specs=(pl.BlockSpec(memory_space=pltpu.VMEM),) * 2,
         scratch_shapes=[
+            pltpu.SMEM(sector_sizes.shape, jnp.int32),
+            pltpu.SMEM(term_links.shape, jnp.int32),
             pltpu.VMEM((block, block), BF16),
             pltpu.VMEM((block, block), BF16),
-            pltpu.VMEM((terms, block, block), BF16),
-            pltpu.VMEM((ONSITE, block, block), BF16),
+            pltpu.VMEM((block, terms * block), BF16),
+            pltpu.VMEM((ONSITE, block, chunks[0][1]), BF16),
+            pltpu.VMEM((block, ONSITE * chunks[1][1]), BF16),
             pltpu.VMEM((count, HOPS, block, chunks[0][1]), BF16),
-            pltpu.VMEM((count, HOPS, block, chunks[1][1]), BF16),
+            pltpu.VMEM((count, block, HOPS * chunks[1][1]), BF16),
             pltpu.VMEM((count, block, block), BF16),
             pltpu.VMEM((count, block, chunks[0][1]), BF16),
             pltpu.VMEM((count, block, chunks[1][1]), BF16),
@@ -250,8 +311,10 @@
             pltpu.VMEM((8, 128), F32),
             pltpu.VMEM((sectors, 8, 128), F32),
             dma((3,)),
-            dma((count, 2)),
-            dma((count, 2)),
+            dma((terms,)),
+            dma((2, ONSITE)),
+            dma((count, 2, HOPS)),
+            dma((count, 2, HOPS)),
             dma((count,)),
             dma((count,)),
             dma((count, 2)),
@@ -260,7 +323,7 @@
             dma((sectors,)),
         ],
         compiler_params=pltpu.CompilerParams(
-            collective_id=0, has_side_effects=True, vmem_limit_bytes=40 * 1024 * 1024
+            collective_id=0, has_side_effects=True, vmem_limit_bytes=int(63.0 * 1024 * 1024)
         ),
         cost_estimate=pl.CostEstimate(
             flops=8 * terms * block**3, bytes_accessed=4 * terms * block * block, transcendentals=0

time: 89.6 us -> 86 us (0.960)
  local copies, waits for them, and re-layouts: 8.37 us -> 3.41 us
  Pallas kernels: 80.3 us -> 81.7 us
    unnamed x12 -> x2, local copies, waits for them, and re-layouts: 8.37 us -> 3.41 us
    pallas_call x1, Pallas kernels: 80.3 us -> 81.7 us  [on_device(): pl.pallas_call(functools.partial(kernel, sectors, chunks), out_shape=(jax...]
where the time goes in v2:
time: 86 us; the launch traced here: 85.8 us
  Pallas kernels  81.7 us (95%)
  local copies, waits for them, and re-layouts  3.41 us (4%)
    pallas_call x1, Pallas kernels, on_device(): pl.pallas_call(functools.partial(kernel, sectors, chunks), out_shape=(jax...  81.7 us
    unnamed x2, local copies, waits for them, and re-layouts  3.41 us

profile of v2, /device:TPU:1, one launch (start us, length us, event | category | flops | bytes accessed | tf_op | source)
XLA Modules:
  0.0 85.8 jit_solution(12048586118991050164)
XLA Ops:
  0.6 81.7 %shard_map.68 = (bf16[1,384,384]{2,1,0:T(8,128)(2,1)}, bf16[1,384,384]{2,1,0:T(8,128)(2,1)}) custom-call(s32[1,2]{1,0:T(1,128)} %sizes_hbm.1, s32[1,16]{1,0:T(1,128)} %links_hbm.1, bf16[1,384,384]{2,1,0:T(8,128)(2,1)} %wave_hbm.1, bf16[1,16,384,384]{3,2,1,0:T(8,128)(2,1)} %left_hbm.1, bf16[1,16,384,384]{3,2,1,0:T(8,128)(2,1)} %right_hbm.1), custom_call_target="tpu_custom_call" | custom-call | flops 7247757312 | bytes 9437184 | tf_op jit(solution)/shard_map/pallas_call | solution.py:292
  82.4 1.7 %copy.9 = bf16[1,384,384]{2,1,0:T(8,128)(2,1)} copy(bf16[1,384,384]{2,1,0:T(8,128)(2,1)} %get-tuple-element.4) | data formatting | bytes 589824
  84.1 1.7 %copy.10 = bf16[1,384,384]{2,1,0:T(8,128)(2,1)} copy(bf16[1,384,384]{2,1,0:T(8,128)(2,1)} %get-tuple-element.5) | data formatting | bytes 589824

commit v3 on v2

--- a/solution.py
+++ b/solution.py
@@ -41,9 +41,10 @@
 
 def kernel(
     sectors, chunks, sizes_hbm, links_hbm, wave_hbm, left_hbm, right_hbm,
+    first_hbm, second_hbm,
     first_out, second_out,
     sizes_ref, links_ref, wave, vec, left, right_on0, right_on1, right_hop0, right_hop1, vec_hop, app_hop0, app_hop1, acc_ref, stat_src, stats,
-    local_sem, left_sem, on_sem, right_send, right_recv, vec_send, vec_recv, app_send, app_recv, stat_send, stat_recv,
+    local_sem, out_sem, left_sem, on_sem, right_send, right_recv, vec_send, vec_recv, app_send, app_recv, stat_send, stat_recv,
 ):
     me = lax.axis_index("sec")
     block = wave.shape[0]
@@ -51,8 +52,8 @@
     right_hop = (right_hop0, right_hop1)
     app_hop = (app_hop0, app_hop1)
 
+    wide, narrow = chunks[0][1], chunks[1][1]
     count = len(slots)
-    wide, narrow = chunks[0][1], chunks[1][1]
     load_wave = pltpu.make_async_copy(wave_hbm.at[0], wave, local_sem.at[0])
     load_sizes = pltpu.make_async_copy(sizes_hbm, sizes_ref, local_sem.at[1])
     load_links = pltpu.make_async_copy(links_hbm, links_ref, local_sem.at[2])
@@ -175,6 +176,17 @@
         region = (rows < rows_live) & (at < cols_live)
         out_ref[0, :, cols] = jnp.where(region, acc_ref[:, cols], 0.0).astype(BF16)
 
+    def sums(c, about):
+        start, width = chunks[c]
+        v = vec[:, pl.ds(start, width)].astype(F32)
+        a = first_out[0, :, pl.ds(start, width)].astype(F32)
+        corr = jnp.sum(v * a, keepdims=True)
+        norm = jnp.sum(v * v, keepdims=True)
+        if about is None:
+            return corr, norm, None, None
+        off = a - about * v
+        return corr, norm, jnp.sum(off * off, keepdims=True), jnp.sum(off * v, keepdims=True)
+
     for c in range(2):
         onsite(vec, c)
     for s in near:
@@ -203,26 +215,27 @@
 
             when(slots[s][1])(arrived)
         finish(first_out, c)
+        if c == 1:
+            for s in near:
+                when(slots[s][3])(lambda s=s: app_copy(s, 1).start())
+            break
         for s in order:
-            def send(s=s, c=c):
-                if c == 0 and s >= 2:
-                    right_sent(s, 1)
-                app_copy(s, c).start()
+            def send(s=s):
+                if s < 2:
+                    app_copy(s, 0).start()
 
             when(slots[s][3])(send)
-
-    v = vec[...].astype(F32)
-    a = first_out[0].astype(F32)
-    corr = jnp.sum(v * a)
-    norm = jnp.sum(v * v)
-    local = jnp.full((1, 1), corr, F32) / (jnp.full((1, 1), norm, F32) + 1e-06)
-    off = a - local * v
-    square = jnp.sum(off * off)
-    cross = jnp.sum(off * v)
-    row = lax.broadcasted_iota(jnp.int32, (8, 128), 0)
-    tile = jnp.where(row == 0, corr, jnp.where(row == 1, norm, jnp.where(row == 2, square, cross)))
-    stat_src[...] = jnp.where(row == 4, jnp.broadcast_to(local, (8, 128)), tile)
-    stats[me] = stat_src[...]
+        corr, norm, _, _ = sums(c, None)
+        local = corr / (norm + 1e-06)
+        first_sums = sums(c, local)
+
+    corr, norm, square, cross = (x + y for x, y in zip(first_sums, sums(1, local)))
+    lane = lax.broadcasted_iota(jnp.int32, (1, 128), 1)
+    tile = jnp.where(lane == 4, local, cross)
+    for i, value in enumerate((corr, norm, square)):
+        tile = jnp.where(lane == i, value, tile)
+    stat_src[...] = tile
+    stats[me] = tile
 
     def stat_copy(peer, slot):
         return remote(stat_src, stats.at[slot], stat_send.at[peer], stat_recv.at[slot], peer)
@@ -230,6 +243,15 @@
     @pl.loop(1, sectors)
     def _(i):
         stat_copy(lax.rem(me + i, sectors), me).start()
+
+    for s in far:
+        def late(s=s):
+            app_copy(s, 0).start()
+            app_copy(s, 1).start()
+
+        when(slots[s][3])(late)
+    first_write = pltpu.make_async_copy(first_out, first_hbm, out_sem.at[0])
+    first_write.start()
 
     @pl.loop(1, sectors)
     def _(i):
@@ -237,7 +259,7 @@
         stat_copy(peer, peer).wait_recv()
 
     def column(i):
-        return stats[:, i : i + 1, :]
+        return jnp.sum(jnp.where(lane[None] == i, stats[...], 0.0), axis=2, keepdims=True)
 
     corr_all = jnp.sum(column(0), axis=0)
     norm_all = jnp.sum(column(1), axis=0)
@@ -245,9 +267,9 @@
     gap = ray[None] - column(4)
     spread = jnp.sum(column(2) - 2.0 * gap * column(3) + gap * gap * column(1), axis=0)
     scale = lax.rsqrt(jnp.maximum(spread, 0.0) / float(sectors * block * block) + 1e-06)
-    ray = ray[:, 0:1]
-    scale = scale[:, 0:1]
-
+
+    v = vec[...].astype(F32)
+    a = first_out[0].astype(F32)
     wave[...] = ((a - ray * v) * scale).astype(BF16)
     for c in range(2):
         onsite(wave, c)
@@ -263,15 +285,23 @@
                 hop(s, c)
 
         when(slots[s][1])(again)
+    second_writes = []
     for c in range(2):
+        start, width = chunks[c]
         finish(second_out, c)
+        second_writes.append(
+            pltpu.make_async_copy(
+                second_out.at[:, :, pl.ds(start, width)], second_hbm.at[:, :, pl.ds(start, width)], out_sem.at[1 + c]
+            )
+        )
+        second_writes[c].start()
 
     for s in order:
         def drain(s=s):
             vec_copy(s).wait_send()
             if s < 2:
                 right_sent(s, 0)
-                right_sent(s, 1)
+            right_sent(s, 1)
             for c in range(2):
                 app_copy(s, c).wait_send()
 
@@ -280,6 +310,40 @@
     @pl.loop(1, sectors)
     def _(i):
         stat_copy(lax.rem(me + i, sectors), me).wait_send()
+
+    first_write.wait()
+    for write in second_writes:
+        write.wait()
+
+
+def settle_kernel(first_in, second_in, first_hbm, second_hbm, held, sem):
+    inward = [
+        pltpu.make_async_copy(first_in, held.at[0], sem.at[0]),
+        pltpu.make_async_copy(second_in, held.at[1], sem.at[1]),
+    ]
+    outward = [
+        pltpu.make_async_copy(held.at[0], first_hbm, sem.at[2]),
+        pltpu.make_async_copy(held.at[1], second_hbm, sem.at[3]),
+    ]
+    for copy in inward:
+        copy.start()
+    for i in range(2):
+        inward[i].wait()
+        outward[i].start()
+    for copy in outward:
+        copy.wait()
+
+
+def settle(first, second):
+    hbm = pl.BlockSpec(memory_space=pltpu.HBM)
+    return pl.pallas_call(
+        settle_kernel,
+        out_shape=(jax.ShapeDtypeStruct(first.shape, BF16),) * 2,
+        in_specs=[hbm, hbm],
+        out_specs=(hbm, hbm),
+        scratch_shapes=[pltpu.VMEM((2,) + first.shape, BF16), pltpu.SemaphoreType.DMA((4,))],
+        compiler_params=pltpu.CompilerParams(vmem_limit_bytes=63 * 1024 * 1024),
+    )(first, second)
 
 
 def on_device(sectors, wavefunction, left_env, right_env, sector_sizes, term_links):
@@ -289,12 +353,14 @@
     chunks = ((0, split), (split, block - split))
     count = 3 if sectors == 2 * ND else 4
     dma = pltpu.SemaphoreType.DMA
-    return pl.pallas_call(
+    first, second = pl.pallas_call(
         functools.partial(kernel, sectors, chunks),
         out_shape=(jax.ShapeDtypeStruct((1, block, block), BF16),) * 2,
         in_specs=[pl.BlockSpec(memory_space=pltpu.HBM)] * 5,
-        out_specs=(pl.BlockSpec(memory_space=pltpu.VMEM),) * 2,
+        out_specs=(pl.BlockSpec(memory_space=pltpu.HBM),) * 2,
         scratch_shapes=[
+            pltpu.VMEM((1, block, block), BF16),
+            pltpu.VMEM((1, block, block), BF16),
             pltpu.SMEM(sector_sizes.shape, jnp.int32),
             pltpu.SMEM(term_links.shape, jnp.int32),
             pltpu.VMEM((block, block), BF16),
@@ -308,8 +374,9 @@
             pltpu.VMEM((count, block, chunks[0][1]), BF16),
             pltpu.VMEM((count, block, chunks[1][1]), BF16),
             pltpu.VMEM((block, block), F32),
-            pltpu.VMEM((8, 128), F32),
-            pltpu.VMEM((sectors, 8, 128), F32),
+            pltpu.VMEM((1, 128), F32),
+            pltpu.VMEM((sectors, 1, 128), F32),
+            dma((3,)),
             dma((3,)),
             dma((terms,)),
             dma((2, ONSITE)),
@@ -329,6 +396,7 @@
             flops=8 * terms * block**3, bytes_accessed=4 * terms * block * block, transcendentals=0
         ),
     )(sector_sizes, term_links, wavefunction, left_env, right_env)
+    return settle(first, second)
 
 
 def solution(mesh):

time: 86 us -> 77.3 us (0.90)
  Pallas kernels: 81.7 us -> 76.5 us
  local copies, waits for them, and re-layouts: 3.41 us -> 0 us
    pallas_call x1, Pallas kernels: 81.7 us -> 74.7 us  [on_device(): pl.pallas_call(functools.partial(kernel, sectors, chunks), out_shape=(jax...]
    unnamed x2 -> x0, local copies, waits for them, and re-layouts: 3.41 us -> none
    pallas_call x0 -> x1, Pallas kernels: none -> 1.81 us  [settle(): pl.pallas_call(settle_kernel, out_shape=(jax.ShapeDtypeStruct(first.shape...]
where the time goes in v3:
time: 77.3 us; the launch traced here: 77.1 us
  Pallas kernels  76.5 us (99%)
    pallas_call x1, Pallas kernels, on_device(): pl.pallas_call(functools.partial(kernel, sectors, chunks), out_shape=(jax...  74.7 us
    pallas_call x1, Pallas kernels, settle(): pl.pallas_call(settle_kernel, out_shape=(jax.ShapeDtypeStruct(first.shape...  1.81 us

profile of v3, /device:TPU:1, one launch (start us, length us, event | category | flops | bytes accessed | tf_op | source)
XLA Modules:
  0.0 77.1 jit_solution(11233138068244860315)
XLA Ops:
  0.6 74.7 %shard_map.68 = (bf16[1,384,384]{2,1,0:T(8,128)(2,1)}, bf16[1,384,384]{2,1,0:T(8,128)(2,1)}) custom-call(s32[1,2]{1,0:T(1,128)} %sizes_hbm.1, s32[1,16]{1,0:T(1,128)} %links_hbm.1, bf16[1,384,384]{2,1,0:T(8,128)(2,1)} %wave_hbm.1, bf16[1,16,384,384]{3,2,1,0:T(8,128)(2,1)} %left_hbm.1, bf16[1,16,384,384]{3,2,1,0:T(8,128)(2,1)} %right_hbm.1), custom_call_target="tpu_custom_call" | custom-call | flops 7247757312 | bytes 9437184 | tf_op jit(solution)/shard_map/pallas_call | solution.py:356
  75.3 1.8 %shard_map.69 = (bf16[1,384,384]{2,1,0:T(8,128)(2,1)}, bf16[1,384,384]{2,1,0:T(8,128)(2,1)}) custom-call(bf16[1,384,384]{2,1,0:T(8,128)(2,1)} %get-tuple-element.4.first_in, bf16[1,384,384]{2,1,0:T(8,128)(2,1)} %get-tuple-element.5.second_in), custom_call_target="tpu_custom_call" | custom-call | tf_op jit(solution)/shard_map/pallas_call | solution.py:339

commit v4 on v3

--- a/solution.py
+++ b/solution.py
@@ -43,14 +43,13 @@
     sectors, chunks, sizes_hbm, links_hbm, wave_hbm, left_hbm, right_hbm,
     first_hbm, second_hbm,
     first_out, second_out,
-    sizes_ref, links_ref, wave, vec, left, right_on0, right_on1, right_hop0, right_hop1, vec_hop, app_hop0, app_hop1, acc_ref, stat_src, stats,
+    sizes_ref, links_ref, wave, vec, left, right_on0, right_on1, right_hop0, right_hop1, vec_hop, app_hop, acc_ref, stat_src, stats,
     local_sem, out_sem, left_sem, on_sem, right_send, right_recv, vec_send, vec_recv, app_send, app_recv, stat_send, stat_recv,
 ):
     me = lax.axis_index("sec")
     block = wave.shape[0]
     slots = hop_slots(me, sectors)
     right_hop = (right_hop0, right_hop1)
-    app_hop = (app_hop0, app_hop1)
 
     wide, narrow = chunks[0][1], chunks[1][1]
     count = len(slots)
@@ -113,11 +112,13 @@
     def vec_copy(s):
         return remote(vec, vec_hop.at[s], vec_send.at[s], vec_recv.at[s], slots[s][2])
 
-    def app_copy(s, c):
-        start, width = chunks[c]
+    pieces = ((0, narrow), (narrow, wide - narrow), (wide, narrow))
+
+    def app_copy(s, p):
+        start, width = pieces[p]
         return remote(
-            first_out.at[0, :, pl.ds(start, width)],
-            app_hop[c].at[s], app_send.at[s, c], app_recv.at[s, c], slots[s][2],
+            first_out.at[0, :, pl.ds(start, width)], app_hop.at[s, :, pl.ds(start, width)],
+            app_send.at[s, p], app_recv.at[s, p], slots[s][2],
         )
 
     order = list(range(len(slots)))[::-1]
@@ -147,12 +148,15 @@
     for copy in rest:
         copy.wait()
 
-    def terms(vector, rights, base, number, c):
+    def terms(vector, rights, base, number, c, skip=0):
         if c == 0:
             raw = [jnp.dot(vector, rights[j], preferred_element_type=F32) for j in range(number)]
         else:
-            side = jnp.dot(vector, rights[...], preferred_element_type=F32)
+            side = jnp.dot(
+                vector, rights[:, pl.ds(skip * narrow, number * narrow)], preferred_element_type=F32
+            )
             raw = [side[:, j * narrow : (j + 1) * narrow] for j in range(number)]
+        base = base + skip
         products = [(raw[j] * links_ref[0, base + j].astype(F32)).astype(BF16) for j in range(number)]
         at = pl.multiple_of(base * block, 128) if not isinstance(base, int) else base * block
         return jnp.dot(
@@ -164,9 +168,9 @@
         rights = right_on0 if c == 0 else right_on1
         acc_ref[:, pl.ds(start, width)] = terms(vector_ref[...], rights, 0, ONSITE, c)
 
-    def hop(s, c):
-        start, width = chunks[c]
-        acc_ref[:, pl.ds(start, width)] += terms(vec_hop[s], right_hop[c].at[s], slots[s][4], HOPS, c)
+    def hop(s, c, number=HOPS, skip=0):
+        start, width = chunks[c]
+        acc_ref[:, pl.ds(start, width)] += terms(vec_hop[s], right_hop[c].at[s], slots[s][4], number, c, skip)
 
     def finish(out_ref, c):
         start, width = chunks[c]
@@ -207,22 +211,34 @@
     for c in range(2):
         for s in far:
             def arrived(s=s, c=c):
+                copies = right_copies(s, c)
                 if c == 0:
                     vec_copy(s).wait_recv()
-                for copy in right_copies(s, c):
-                    copy.wait_recv()
-                hop(s, c)
+                    for copy in copies:
+                        copy.wait_recv()
+                    hop(s, c)
+                else:
+                    for copy in copies[:-1]:
+                        copy.wait_recv()
+                    hop(s, c, HOPS - 1)
+                    copies[-1].wait_recv()
 
             when(slots[s][1])(arrived)
+        if c == 1:
+            for s in far:
+                when(slots[s][3])(lambda s=s: app_copy(s, 0).start())
+            for s in far:
+                when(slots[s][1])(lambda s=s: hop(s, 1, 1, HOPS - 1))
         finish(first_out, c)
         if c == 1:
             for s in near:
-                when(slots[s][3])(lambda s=s: app_copy(s, 1).start())
+                when(slots[s][3])(lambda s=s: app_copy(s, 2).start())
             break
         for s in order:
             def send(s=s):
                 if s < 2:
                     app_copy(s, 0).start()
+                    app_copy(s, 1).start()
 
             when(slots[s][3])(send)
         corr, norm, _, _ = sums(c, None)
@@ -246,8 +262,8 @@
 
     for s in far:
         def late(s=s):
-            app_copy(s, 0).start()
             app_copy(s, 1).start()
+            app_copy(s, 2).start()
 
         when(slots[s][3])(late)
     first_write = pltpu.make_async_copy(first_out, first_hbm, out_sem.at[0])
@@ -275,12 +291,10 @@
         onsite(wave, c)
     for s in range(count):
         def again(s=s):
-            for c in range(2):
-                start, width = chunks[c]
-                cols = pl.ds(start, width)
-                app_copy(s, c).wait_recv()
-                before = vec_hop[s, :, cols].astype(F32)
-                vec_hop[s, :, cols] = ((app_hop[c][s].astype(F32) - ray * before) * scale).astype(BF16)
+            for p in range(3):
+                app_copy(s, p).wait_recv()
+            before = vec_hop[s].astype(F32)
+            vec_hop[s] = ((app_hop[s].astype(F32) - ray * before) * scale).astype(BF16)
             for c in range(2):
                 hop(s, c)
 
@@ -302,8 +316,8 @@
             if s < 2:
                 right_sent(s, 0)
             right_sent(s, 1)
-            for c in range(2):
-                app_copy(s, c).wait_send()
+            for p in range(3):
+                app_copy(s, p).wait_send()
 
         when(slots[s][3])(drain)
 
@@ -371,8 +385,7 @@
             pltpu.VMEM((count, HOPS, block, chunks[0][1]), BF16),
             pltpu.VMEM((count, block, HOPS * chunks[1][1]), BF16),
             pltpu.VMEM((count, block, block), BF16),
-            pltpu.VMEM((count, block, chunks[0][1]), BF16),
-            pltpu.VMEM((count, block, chunks[1][1]), BF16),
+            pltpu.VMEM((count, block, block), BF16),
             pltpu.VMEM((block, block), F32),
             pltpu.VMEM((1, 128), F32),
             pltpu.VMEM((sectors, 1, 128), F32),
@@ -384,8 +397,8 @@
             dma((count, 2, HOPS)),
             dma((count,)),
             dma((count,)),
-            dma((count, 2)),
-            dma((count, 2)),
+            dma((count, 3)),
+            dma((count, 3)),
             dma((sectors,)),
             dma((sectors,)),
         ],

time: 77.3 us -> 77.2 us (level)
  no operation moved by 1% of the time
where the time goes in v4:
time: 77.2 us; the launch traced here: 76.5 us
  Pallas kernels  75.9 us (98%)
    pallas_call x1, Pallas kernels, on_device(): pl.pallas_call(functools.partial(kernel, sectors, chunks), out_shape=(jax...  74.1 us
    pallas_call x1, Pallas kernels, settle(): pl.pallas_call(settle_kernel, out_shape=(jax.ShapeDtypeStruct(first.shape...  1.81 us

profile of v4, /device:TPU:1, one launch (start us, length us, event | category | flops | bytes accessed | tf_op | source)
XLA Modules:
  0.0 76.5 jit_solution(17572920093611657585)
XLA Ops:
  0.6 74.1 %shard_map.68 = (bf16[1,384,384]{2,1,0:T(8,128)(2,1)}, bf16[1,384,384]{2,1,0:T(8,128)(2,1)}) custom-call(s32[1,2]{1,0:T(1,128)} %sizes_hbm.1, s32[1,16]{1,0:T(1,128)} %links_hbm.1, bf16[1,384,384]{2,1,0:T(8,128)(2,1)} %wave_hbm.1, bf16[1,16,384,384]{3,2,1,0:T(8,128)(2,1)} %left_hbm.1, bf16[1,16,384,384]{3,2,1,0:T(8,128)(2,1)} %right_hbm.1), custom_call_target="tpu_custom_call" | custom-call | flops 7247757312 | bytes 9437184 | tf_op jit(solution)/shard_map/pallas_call | solution.py:370
  74.7 1.8 %shard_map.69 = (bf16[1,384,384]{2,1,0:T(8,128)(2,1)}, bf16[1,384,384]{2,1,0:T(8,128)(2,1)}) custom-call(bf16[1,384,384]{2,1,0:T(8,128)(2,1)} %get-tuple-element.4.first_in, bf16[1,384,384]{2,1,0:T(8,128)(2,1)} %get-tuple-element.5.second_in), custom_call_target="tpu_custom_call" | custom-call | tf_op jit(solution)/shard_map/pallas_call | solution.py:353
